TPU v7x, 512 devices: a whole 4x8x8 slice. The times are simulated.
512 devices in a mesh: ctx: 64 (over z, y), kv: 8 (over x, core).
Axes of the slice: x: 4, y: 8, z: 8, core: 2. Of those that a mesh axis runs over, the one named last changes fastest.
Arguments:
- hidden: bfloat16 [2, 8, 8192], P(None, None, 'ctx'), may hold values from -6 to 6
- w_qkv: bfloat16 [8192, 10240], P('ctx', 'kv'), may hold values from -0.0625 to 0.0625
- w_out: bfloat16 [8192, 8192], P('kv', 'ctx'), may hold values from -0.5 to 0.5
- key_pages: bfloat16 [8, 2048, 16, 1024], P(None, 'ctx', None, 'kv'), may hold values from -320 to 320
- value_pages: bfloat16 [8, 2048, 16, 1024], P(None, 'ctx', None, 'kv'), may hold values from -6 to 6
- ctx_len: int32 [8], replicated, may hold values from 4096 to 32768, as said below
- selected: int32 [2, 8, 8, 256], P(None, None, 'kv'), may hold values from 0 to 2047, as said below
- tail_keys: bfloat16 [4096, 16, 1024], P('ctx', None, 'kv'), may hold values from -8 to 8
- tail_values: bfloat16 [4096, 16, 1024], P('ctx', None, 'kv'), may hold values from -6 to 6
- tail_count: int32 [8], replicated, may hold values from 1 to 1024, 4096 in all
- tail_dest: int32 [4096, 1], replicated, may hold values from 0 to 63; in each aligned block of 64 rows (0 to 63, 64 to 127, ...) at most 2 rows name the same one
Outputs:
- mixed: bfloat16 [2, 8, 8192], P(None, None, 'ctx')
- stored_keys: bfloat16 [8192, 16, 1024], P('ctx', None, 'kv')
- stored_values: bfloat16 [8192, 16, 1024], P('ctx', None, 'kv')
- stored_bounds: bfloat16 [8192, 2, 1024], P('ctx', None, 'kv')
Inputs may be any that keep to these rules, and one draw needn't show every extreme that they name: `ctx_len`: some row has exactly 32768 tokens. `selected`: 256 different page numbers for each step, row and key-value head, each below ceil(ctx_len of the row / 16). `tail_count`: the counts add up to 4096; the largest is exactly 1024. `tail_dest`: among the 64 tail pages of one device, at most 2 name one owner, a bound that some block reaches.
All inputs are finite; a program needn't handle non-finite values.
Results may differ from a plain program's by a relative error of at most 0.012.
The roundings to bfloat16 on the way count: a program that leaves them out, or rounds other values in their place, can miss the bound.
Values may be sent and summed in bfloat16 or wider, within the bound.
A program may use at most 64 MiB of HBM per device.

v0:
```python
import math

import jax
import jax.numpy as jnp
from jax import lax
from jax.sharding import PartitionSpec as P

HQ = 64
KVH = 8
HD = 128
PAIR = 2


neg_big = -1e30
highest = lax.Precision.HIGHEST


def page_scores(queries, page_keys, page_rows, page_live):
    row_count = queries.shape[1]
    head_count = queries.shape[2]
    head_width = queries.shape[4]
    page_count = page_keys.shape[0]
    keys_four = page_keys.reshape(page_count, page_keys.shape[1], head_count, head_width)
    page_query = jnp.take(queries, jnp.clip(page_rows, 0, row_count - 1), axis=1)
    scores = jnp.einsum(
        "sphgd,pthd->sphgt", page_query, keys_four, preferred_element_type=jnp.float32
    ) * (1.0 / math.sqrt(head_width))
    scores = jnp.where(page_live[None, :, None, None, None], scores, neg_big)
    member = (page_rows[None, :] == jnp.arange(row_count)[:, None]) & page_live[None, :]
    page_peak = jnp.max(scores, axis=-1)
    row_peak = jnp.max(
        jnp.where(member[None, :, :, None, None], page_peak[:, None], neg_big), axis=2
    )
    return (scores, member, row_peak)


def page_sums(scores, member, global_peak, page_rows, page_values):
    row_count = global_peak.shape[1]
    head_count = global_peak.shape[2]
    page_count = page_values.shape[0]
    values_four = page_values.reshape(page_count, page_values.shape[1], head_count, -1)
    page_peak = jnp.take(global_peak, jnp.clip(page_rows, 0, row_count - 1), axis=1)
    weights = jnp.exp(scores - page_peak[..., None])
    totals = jnp.sum(weights, axis=-1)
    weighted = jnp.einsum(
        "sphgt,pthd->sphgd",
        weights.astype(jnp.bfloat16),
        values_four,
        preferred_element_type=jnp.float32,
    )
    onehot = member.astype(jnp.float32)
    row_totals = jnp.einsum("rp,sphg->srhg", onehot, totals, precision=highest)
    row_weighted = jnp.einsum("rp,sphgd->srhgd", onehot, weighted, precision=highest)
    return (row_totals, row_weighted)


def on_device(
    hidden,
    w_qkv,
    w_out,
    key_pages,
    value_pages,
    ctx_len,
    selected,
    tail_keys,
    tail_values,
    tail_count,
    tail_dest,
):
    step_count, row_count, local_width = hidden.shape
    head_count = key_pages.shape[3] // HD
    group_size = HQ // KVH
    page_len = key_pages.shape[2]
    pages_here = key_pages.shape[1]
    out_here = tail_keys.shape[0]
    feature = tail_keys.shape[2]
    ctx_count = lax.axis_size("ctx")
    ctx_rank = lax.axis_index("ctx")
    score_scale = 1.0 / math.sqrt(HD)
    partial_qkv = jnp.dot(
        hidden.reshape(step_count * row_count, local_width),
        w_qkv,
        preferred_element_type=jnp.float32,
    )
    projected = lax.psum(partial_qkv, "ctx")
    projected = projected.astype(jnp.bfloat16).reshape(
        step_count, row_count, head_count, group_size + 2, HD
    )
    queries = projected[:, :, :, :group_size]
    new_keys = projected[:, :, :, group_size]
    new_values = projected[:, :, :, group_size + 1]
    dest_all = tail_dest[:, 0].reshape(ctx_count, out_here)
    owner_hot = (
        dest_all[:, :, None] == jnp.arange(ctx_count, dtype=jnp.int32)[None, None, :]
    ).astype(jnp.int32)
    before = jnp.cumsum(owner_hot, axis=1) - owner_hot
    rank_all = jnp.sum(before * owner_hot, axis=2)
    row_ends = jnp.cumsum(tail_count)
    slot_ids = jnp.arange(ctx_count * out_here, dtype=jnp.int32)
    rows_all = jnp.sum((slot_ids[:, None] >= row_ends[None, :]).astype(jnp.int32), axis=1).reshape(
        ctx_count, out_here
    )
    my_dest = lax.dynamic_index_in_dim(dest_all, ctx_rank, 0, keepdims=False)
    my_rank = lax.dynamic_index_in_dim(rank_all, ctx_rank, 0, keepdims=False)
    target = my_dest * PAIR + my_rank
    placing = (jnp.arange(ctx_count * PAIR, dtype=jnp.int32)[:, None] == target[None, :]).astype(
        jnp.bfloat16
    )
    send_keys = jnp.dot(
        placing, tail_keys.reshape(out_here, -1), preferred_element_type=jnp.float32
    )
    send_keys = send_keys.astype(jnp.bfloat16).reshape(ctx_count, PAIR, page_len, feature)
    send_values = jnp.dot(
        placing, tail_values.reshape(out_here, -1), preferred_element_type=jnp.float32
    )
    send_values = send_values.astype(jnp.bfloat16).reshape(ctx_count, PAIR, page_len, feature)
    bounds = jnp.stack([jnp.min(tail_keys, axis=1), jnp.max(tail_keys, axis=1)], axis=1)
    send_bounds = jnp.dot(placing, bounds.reshape(out_here, -1), preferred_element_type=jnp.float32)
    send_bounds = send_bounds.astype(jnp.bfloat16).reshape(ctx_count, PAIR, 2, feature)
    got_keys, got_values, got_bounds = (
        lax.all_to_all(send_keys, "ctx", split_axis=0, concat_axis=0, tiled=True),
        lax.all_to_all(send_values, "ctx", split_axis=0, concat_axis=0, tiled=True),
        lax.all_to_all(send_bounds, "ctx", split_axis=0, concat_axis=0, tiled=True),
    )
    stored_bounds = got_bounds.reshape(ctx_count * PAIR, 2, feature)
    stored_keys = got_keys.reshape(ctx_count * PAIR, page_len, feature)
    stored_values = got_values.reshape(ctx_count * PAIR, page_len, feature)
    keys_five = key_pages.reshape(row_count, pages_here, page_len, head_count, HD)
    values_five = value_pages.reshape(row_count, pages_here, page_len, head_count, HD)
    resident_scores = (
        jnp.einsum("srhgd,rjthd->srhgjt", queries, keys_five, preferred_element_type=jnp.float32)
        * score_scale
    )
    page_ids = ctx_rank * pages_here + jnp.arange(pages_here, dtype=jnp.int32)
    chosen = jnp.any(selected[..., None] == page_ids, axis=3)
    positions = page_ids[:, None] * page_len + jnp.arange(page_len, dtype=jnp.int32)[None, :]
    inside = positions[None] < ctx_len[:, None, None]
    keep_mask = chosen[:, :, :, None, :, None] & inside[None, :, None, None, :, :]
    resident_scores = jnp.where(keep_mask, resident_scores, neg_big)
    resident_peak = jnp.max(resident_scores, axis=(4, 5))
    mine_mask = dest_all == ctx_rank
    slot_hit = mine_mask[:, :, None] & (
        rank_all[:, :, None] == jnp.arange(PAIR, dtype=jnp.int32)[None, None, :]
    )
    page_live = jnp.any(slot_hit, axis=1).reshape(-1)
    page_rows = jnp.sum(jnp.where(slot_hit, rows_all[:, :, None], 0), axis=1).reshape(-1)
    tail_scores, member, tail_peak = page_scores(queries, stored_keys, page_rows, page_live)
    own_scores = (
        jnp.einsum("srhgd,urhd->srhgu", queries, new_keys, preferred_element_type=jnp.float32)
        * score_scale
    )
    causal = jnp.arange(step_count)[:, None] >= jnp.arange(step_count)[None, :]
    own_scores = jnp.where(causal[:, None, None, None, :], own_scores, neg_big)
    local_peak = jnp.maximum(resident_peak, tail_peak)
    global_peak = jnp.maximum(lax.pmax(local_peak, "ctx"), jnp.max(own_scores, axis=-1))
    resident_weights = jnp.exp(resident_scores - global_peak[..., None, None])
    resident_totals = jnp.sum(resident_weights, axis=(4, 5))
    resident_weighted = jnp.einsum(
        "srhgjt,rjthd->srhgd",
        resident_weights.astype(jnp.bfloat16),
        values_five,
        preferred_element_type=jnp.float32,
    )
    tail_totals, tail_weighted = page_sums(
        tail_scores, member, global_peak, page_rows, stored_values
    )
    totals, weighted = lax.psum(
        (resident_totals + tail_totals, resident_weighted + tail_weighted), "ctx"
    )
    own_weights = jnp.exp(own_scores - global_peak[..., None])
    totals = totals + jnp.sum(own_weights, axis=-1)
    weighted = weighted + jnp.einsum(
        "srhgu,urhd->srhgd",
        own_weights.astype(jnp.bfloat16),
        new_values,
        preferred_element_type=jnp.float32,
    )
    attention = (
        (weighted / totals[..., None])
        .astype(jnp.bfloat16)
        .reshape(step_count * row_count, head_count * group_size * HD)
    )
    summed = lax.psum(jnp.dot(attention, w_out, preferred_element_type=jnp.float32), "kv")
    mixed = summed.astype(jnp.bfloat16).reshape(step_count, row_count, -1)
    return (mixed, stored_keys, stored_values, stored_bounds)


def solution(mesh):
    placed = (
        P(None, None, "ctx"),
        P("ctx", "kv"),
        P("kv", "ctx"),
        P(None, "ctx", None, "kv"),
        P(None, "ctx", None, "kv"),
        P(),
        P(None, None, "kv", None),
        P("ctx", None, "kv"),
        P("ctx", None, "kv"),
        P(),
        P(),
    )
    return jax.shard_map(
        on_device,
        mesh=mesh,
        in_specs=placed,
        out_specs=(
            P(None, None, "ctx"),
            P("ctx", None, "kv"),
            P("ctx", None, "kv"),
            P("ctx", None, "kv"),
        ),
        check_vma=False,
    )
```

profile of v0, /device:TPU:1, one launch (start us, length us, event | category | flops | bytes accessed | tf_op | source)
XLA Modules:
  0.0 806.5 jit_solution(7375697592480430313)
XLA Ops:
  7.2 0.5 broadcast.242
  7.7 1.4 reduce.13
  9.3 2.3 fusion.3
  11.6 1.2 fusion.71
  12.7 0.2 add_reduce_fusion
  12.9 0.2 convolution_convert_fusion.2
  13.1 0.7 reshape.339
  13.7 17.1 %all-to-all-start.2 = ((bf16[64,2,2,128]{3,2,1,0:T(2,128)(2,1)}), bf16[64,2,2,128]{3,2,1,0:T(2,128)(2,1)S(1)}, u32[]{:S(2)}, u32[]{:S(2)}) async-start(bf16[64,2,2,128]{3,2,1,0:T(2,128)(2,1)} %reshape.339), calls=%async_computation.2 | async-start | bytes 131072 | tf_op jit(solution)/shard_map/all_to_all | solution.py:123
  31.0 0.2 reduce-window.8
  31.1 0.1 convert_reduce_fusion
  31.3 0.1 select_reduce_fusion.1
  31.7 0.2 fusion.62
  31.8 224.3 %psum.28 = bf16[16,1280]{1,0:T(8,128)(2,1)S(1)} all-reduce(f32[16,1280]{1,0:T(8,128)S(1)} %fusion.62), channel_id=1, replica_groups=mesh['ctx'=64,'kv'=8] {'ctx'}, use_global_device_ids=true, to_apply=%region_1.0 | all-reduce | flops 20480 | bytes 122880 | tf_op jit(solution)/shard_map/psum | solution.py:85
  256.2 0.3 fusion.9
  256.5 0.9 copy.176
  257.4 0.1 min.20
  257.6 0.1 eq.105
  257.8 0.1 copy.136
  257.9 0.1 and.55
  258.1 0.4 compare_reduce_fusion
  258.5 0.3 fusion.10
  258.8 0.9 copy.178
  259.8 1.5 gather_fusion
  261.3 5.1 all-to-all-start
  266.5 0.3 fusion.75
  266.8 1.6 fusion.74
  268.4 12.6 %all-to-all-done = bf16[64,2,16,128]{3,2,1,0:T(8,128)(2,1)S(1)} async-done(((bf16[64,2,16,128]{3,2,1,0:T(8,128)(2,1)}), bf16[64,2,16,128]{3,2,1,0:T(8,128)(2,1)S(1)}, u32[]{:S(2)}, u32[]{:S(2)}) %all-to-all-start) | async-done | bytes 524320 | tf_op jit(solution)/shard_map/all_to_all | solution.py:121
  281.0 4.6 all-to-all-start.1
  285.7 2.6 fusion.73
  288.5 119.3 %pmax.7 = f32[2,8,1,8]{3,1,0,2:T(8,128)S(1)} all-reduce(f32[2,8,1,8]{3,1,0,2:T(8,128)S(1)} %fusion.60), channel_id=1, replica_groups=mesh['ctx'=64,'kv'=8] {'ctx'}, use_global_device_ids=true, to_apply=%region_11.12 | all-reduce | flops 128 | bytes 1024 | tf_op jit(solution)/shard_map/pmax | solution.py:155
  407.8 0.7 gather_fusion.1
  408.6 0.3 fusion.23
  408.9 0.2 select_bitcast_fusion
  409.1 0.7 copy-done.1
  409.8 0.8 fusion.25
  410.6 0.2 fusion.16
  410.8 112.2 %psum.30 = f32[2,8,1,8]{3,1,0,2:T(8,128)S(1)} all-reduce(f32[2,8,1,8]{3,1,0,2:T(8,128)S(1)} %fusion.16), channel_id=1, replica_groups=mesh['ctx'=64,'kv'=8] {'ctx'}, use_global_device_ids=true, to_apply=%region_16.17 | all-reduce | flops 128 | bytes 1024 | tf_op jit(solution)/shard_map/psum | solution.py:167
  523.0 1.7 convolution_bitcast_fusion
  524.7 0.7 fusion.20
  525.4 0.5 copy-done.2
  525.9 1.3 fusion.11
  527.3 251.1 %all-reduce.2.cloned.1.call-done = f32[2,8,1,8,128]{4,3,0,1,2:T(8,128)} async-done(((f32[2,8,1,8,128]{4,3,0,1,2:T(8,128)}), f32[2,8,1,8,128]{4,3,0,1,2:T(8,128)}) %all-reduce.2.cloned.1.call-update) | async-done | bytes 65552 | tf_op jit(solution)/shard_map/psum | solution.py:167
  778.4 1.0 fusion.14
  779.5 0.2 fusion.44
  779.6 17.8 %psum.31 = bf16[16,128]{1,0:T(8,128)(2,1)} all-reduce(f32[16,128]{1,0:T(8,128)S(1)} %fusion.44), channel_id=1, replica_groups=mesh['ctx'=64,'kv'=8] {'kv'}, use_global_device_ids=true, to_apply=%region_18.19 | all-reduce | flops 2048 | bytes 12288 | tf_op jit(solution)/shard_map/psum | solution.py:183
  797.5 0.8 copy.238
  798.3 0.8 copy.239
  799.1 0.6 copy.240
  (56 shorter events, 1.1 us)
Async XLA Ops:
  7.2 259.7 %copy-start = (bf16[8,32,16,128]{3,2,1,0:T(8,128)(2,1)S(1)}, bf16[8,32,16,128]{3,2,1,0:T(8,128)(2,1)}, u32[]{:S(2)}) copy-start(bf16[8,32,16,128]{3,2,1,0:T(8,128)(2,1)} %param.14) | copy-start | bytes 3145732
  7.2 249.0 %copy-start.3 = (bf16[64,16,128]{2,1,0:T(8,128)(2,1)S(1)}, bf16[64,16,128]{2,1,0:T(8,128)(2,1)}, u32[]{:S(2)}) copy-start(bf16[64,16,128]{2,1,0:T(8,128)(2,1)} %param.18) | copy-start | bytes 786436
  7.2 23.8 %copy-start.10 = (s32[8]{0:T(128)S(1)}, s32[8]{0:T(128)}, u32[]{:S(2)}) copy-start(s32[8]{0:T(128)} %param.20) | copy-start | bytes 100
  7.2 24.5 %copy-start.8 = (bf16[2,8,128]{2,1,0:T(8,128)(2,1)S(1)}, bf16[2,8,128]{2,1,0:T(8,128)(2,1)}, u32[]{:S(2)}) copy-start(bf16[2,8,128]{2,1,0:T(8,128)(2,1)} %param.11) | copy-start | bytes 12292
  7.2 24.5 %copy-start.4 = (bf16[128,1280]{1,0:T(8,128)(2,1)S(1)}, bf16[128,1280]{1,0:T(8,128)(2,1)}, u32[]{:S(2)}) copy-start(bf16[128,1280]{1,0:T(8,128)(2,1)} %param.12) | copy-start | bytes 983044
  13.7 247.5 %all-to-all-start.2 = ((bf16[64,2,2,128]{3,2,1,0:T(2,128)(2,1)}), bf16[64,2,2,128]{3,2,1,0:T(2,128)(2,1)S(1)}, u32[]{:S(2)}, u32[]{:S(2)}) async-start(bf16[64,2,2,128]{3,2,1,0:T(2,128)(2,1)} %reshape.339), calls=%async_computation.2 | async-start | bytes 131072 | tf_op jit(solution)/shard_map/all_to_all | solution.py:123
  256.1 1.9 copy-start.7
  256.1 2.4 copy-start.6
  259.8 6.7 copy-start.9
  261.3 19.7 %all-to-all-start = ((bf16[64,2,16,128]{3,2,1,0:T(8,128)(2,1)}), bf16[64,2,16,128]{3,2,1,0:T(8,128)(2,1)S(1)}, u32[]{:S(2)}, u32[]{:S(2)}) async-start(bf16[64,2,16,128]{3,2,1,0:T(8,128)(2,1)} %bitcast.90), calls=%async_computation | async-start | bytes 1048576 | tf_op jit(solution)/shard_map/all_to_all | solution.py:121
  281.0 242.0 %all-to-all-start.1 = ((bf16[64,2,16,128]{3,2,1,0:T(8,128)(2,1)}), bf16[64,2,16,128]{3,2,1,0:T(8,128)(2,1)S(1)}, u32[]{:S(2)}, u32[]{:S(2)}) async-start(bf16[64,2,16,128]{3,2,1,0:T(8,128)(2,1)} %bitcast.202), calls=%async_computation.1 | async-start | bytes 1048576 | tf_op jit(solution)/shard_map/all_to_all | solution.py:122
  285.6 492.8 %all-reduce.2.cloned.1.call-start = ((), (), s32[]{:S(2)}) async-start(), calls=%async_computation.3 | async-start | bytes 131072 | tf_op jit(solution)/shard_map/psum | solution.py:167
  408.6 1.2 copy-start.1
  524.7 1.2 copy-start.2
  525.9 253.5 %copy-start.5 = (bf16[1024,128]{1,0:T(8,128)(2,1)S(1)}, bf16[1024,128]{1,0:T(8,128)(2,1)}, u32[]{:S(2)}) copy-start(bf16[1024,128]{1,0:T(8,128)(2,1)} %param.13) | copy-start | bytes 786436
Sparse Core Ops, SparseCore 0:
  527.4 250.9 all-reduce.1
where the time goes:
time: 807 us
  blocking collectives  474 us (59%)
  waiting for transfers between devices  264 us (33%)
  starting transfers between devices  26.9 us (3%)
  between operations  14.5 us (2%)
  matrix products  10.4 us (1%)
  local copies, waits for them, and re-layouts  9.78 us (1%)
    psum x1, waiting for transfers between devices, on_device(): lax.psum((resident_totals + tail_totals, resident_weighted + tail_weighte...  251 us
    psum x1, blocking collectives, on_device(): projected = lax.psum(partial_qkv, 'ctx')  224 us
    pmax x1, blocking collectives, on_device(): lax.pmax(local_peak, 'ctx')  119 us
    psum x1, blocking collectives, on_device(): lax.psum((resident_totals + tail_totals, resident_weighted + tail_weighte...  112 us
    psum x1, blocking collectives, on_device(): lax.psum(jnp.dot(attention, w_out, preferred_element_type=jnp.float32), '...  17.8 us
    all_to_all x1, starting transfers between devices, on_device(): lax.all_to_all(send_bounds, 'ctx', split_axis=0, concat_axis=0, tiled=True)  17.1 us
  transfers between devices with their start and end apart: 4, of which 2 were waited for; matrix products, arithmetic and copies ran while one was open for 2% of the time, Pallas kernels for 0%

commit v1 on v0

v1 whole, which is shorter than its diff:
```python
import functools
import math

import jax
import jax.numpy as jnp
from jax import lax
from jax.experimental import pallas as pl
from jax.experimental.pallas import tpu as pltpu
from jax.sharding import PartitionSpec as P

HD = 128
GROUP = 8
PAIR = 2
ROWS = 8
STEPS = 2
PAGE = 16
NZ = 8
QR = STEPS * GROUP
PIECE = 24
NEG = -1e30
MESH = pl.DeviceIdType.MESH
ORDER = (1, 7, 2, 6, 3, 5, 4, 0)
PACE = ((0, 1), (2, 3), (4, 5), (6, 7))


def nt(a, b):
    return lax.dot_general(a, b, (((1,), (1,)), ((), ())), preferred_element_type=jnp.float32)


def nn(a, b):
    return jnp.dot(a, b, preferred_element_type=jnp.float32)


def body(
    ny, nkv, out_here, pages_here,
    ctx_len, tail_count, hidden, w_qkv, w_out, keys, values, selected, tail_k, tail_v, dest,
    mixed, out_k, out_v, out_min, out_max,
    hid_v, wq_v, wo_v, k_v, v_v, sel_v, dest_v, tk_v, tv_v,
    part, ra1, a2s, ra2, qsend, qbuf, bias, bsend, rb1, b2s, rb2, asend, abuf, attf, csend, rc,
    stage, trecv, inv_v, inv_s,
    in_sem, send_sem, za_sem, ya_sem, zq_sem, zb_sem, yb_sem, zt_sem, kv_sem,
    tail_send, tail_recv, out_sem, inv_sem, ready,
):
    ctx = lax.axis_index("ctx")
    kv = lax.axis_index("kv")
    z = lax.div(ctx, ny)
    y = lax.rem(ctx, ny)
    n_ctx = NZ * ny
    score_scale = 1.0 / math.sqrt(HD)
    tokens = pages_here * PAGE
    tail_tokens = out_here * PAGE

    def z_peer(d):
        peer = lax.rem(z + d, NZ)
        return peer, (peer * ny + y, kv)

    def y_peer(d):
        peer = lax.rem(y + d, ny)
        return peer, (z * ny + peer, kv)

    def kv_peer(d):
        peer = lax.rem(kv + d, nkv)
        return peer, (ctx, peer)

    barrier = pltpu.get_barrier_semaphore()
    peers = NZ - 1 + ny - 1 + nkv - 1
    for count, peer_of in ((NZ, z_peer), (ny, y_peer), (nkv, kv_peer)):
        for d in range(1, count):
            pl.semaphore_signal(barrier, inc=1, device_id=peer_of(d)[1], device_id_type=MESH)

    first = lax.div(ctx * out_here, 128) * 128
    loads = [
        (hidden, hid_v),
        (w_qkv, wq_v),
        (dest.at[:, pl.ds(pl.multiple_of(first, 128), 128)], dest_v),
        (tail_k, tk_v.at[pl.ds(0, out_here)]),
        (tail_v, tv_v.at[pl.ds(0, out_here)]),
        (selected, sel_v),
        (keys, k_v),
        (values, v_v),
        (w_out, wo_v),
    ]
    loads = [pltpu.make_async_copy(a, b, in_sem.at[i]) for i, (a, b) in enumerate(loads)]
    for load in loads:
        load.start()

    tk_v[out_here] = jnp.zeros((PAGE, HD), jnp.bfloat16)
    tv_v[out_here] = jnp.zeros((PAGE, HD), jnp.bfloat16)
    loads[2].wait()
    offset = ctx * out_here - first
    sub = lax.broadcasted_iota(jnp.int32, (128, 128), 0)
    lane = lax.broadcasted_iota(jnp.int32, (128, 128), 1)
    lane_mine = (lane >= offset) & (lane < offset + out_here)
    sub_mine = (sub >= offset) & (sub < offset + out_here)
    dest_row = jnp.broadcast_to(dest_v[...], (128, 128))
    dest_col = jnp.sum(jnp.where(sub == lane, dest_row, 0), axis=1, keepdims=True)
    same = (dest_row == dest_col) & lane_mine & (lane < sub)
    rank_col = jnp.sum(jnp.where(same, 1, 0), axis=1, keepdims=True)
    target = dest_col * PAIR + rank_col
    hit = (lane == target) & sub_mine
    table = jnp.sum(jnp.where(hit, sub - offset - out_here, 0), axis=0, keepdims=True) + out_here
    inv_v[...] = jnp.broadcast_to(table, (8, 128))
    table_copy = pltpu.make_async_copy(inv_v, inv_s, inv_sem.at[0])
    table_copy.start()

    loads[0].wait()
    loads[1].wait()
    proj = nn(hid_v[...], wq_v[...])
    for j in range(GROUP + 2):
        for s in range(STEPS):
            at = s * GROUP + j if j < GROUP else QR + (j - GROUP) * STEPS + s
            part[pl.ds(at, ROWS, stride=PIECE), :] = proj[s * ROWS:(s + 1) * ROWS, j * HD:(j + 1) * HD]

    pl.semaphore_wait(barrier, peers)
    for d in range(1, ny):
        pl.semaphore_signal(ready, inc=1, device_id=y_peer(d)[1], device_id_type=MESH)

    def piece(i):
        return pl.ds(pl.multiple_of(i * PIECE, 8), PIECE)

    def q_rows(i):
        return pl.ds(pl.multiple_of(i * QR, QR), QR)

    def exchange(phase, count, peer_of, me, src, dst, recv):
        copies = []
        for d in range(1, count):
            peer, device = peer_of(d)
            copy = pltpu.make_async_remote_copy(
                src_ref=src(peer), dst_ref=dst(me), send_sem=send_sem.at[phase, d], recv_sem=recv.at[me],
                device_id=device, device_id_type=MESH,
            )
            copy.start()
            copies.append(copy)

        def wait():
            for d in range(1, count):
                peer, device = peer_of(d)
                pltpu.make_async_remote_copy(
                    src_ref=src(peer), dst_ref=dst(peer), send_sem=send_sem.at[phase, d], recv_sem=recv.at[peer],
                    device_id=device, device_id_type=MESH,
                ).wait_recv()

        return wait, copies

    sent = []

    def tail_block(distance, i):
        to_z = lax.rem(z + distance, NZ)
        to_y = lax.rem(y + i, ny)
        return pltpu.make_async_remote_copy(
            src_ref=stage.at[to_z * ny + to_y], dst_ref=trecv.at[ctx],
            send_sem=tail_send.at[distance], recv_sem=tail_recv.at[z],
            device_id=(to_z * ny + to_y, kv), device_id_type=MESH,
        )

    def tail_start(batch):
        distance = ORDER[batch]
        if distance == 0:
            pltpu.make_async_copy(stage.at[ctx], trecv.at[ctx], tail_recv.at[z]).start()

        def start(i, carry):
            tail_block(distance, i).start()
            return carry

        lax.fori_loop(1 if distance == 0 else 0, ny, start, 0)

    wait, copies = exchange(0, NZ, z_peer, z, lambda p: part.at[piece(p)], lambda m: ra1.at[m], za_sem)
    sent += copies
    ra1[z] = part[piece(z), :]

    loads[3].wait()
    loads[4].wait()
    table_copy.wait()

    def place(d, carry):
        for k in range(PAIR):
            page = inv_s[0, d * PAIR + k]
            stage[d, 0, k] = tk_v[page]
            stage[d, 1, k] = tv_v[page]
        return carry

    lax.fori_loop(0, n_ctx, place, 0)
    if ny > 1:
        pl.semaphore_wait(ready, ny - 1)
    for batch in PACE[0]:
        tail_start(batch)

    wait()
    a2s[...] = functools.reduce(lambda a, b: a + b, [ra1[i] for i in range(NZ)])
    wait, copies = exchange(1, ny, y_peer, y, lambda p: a2s, lambda m: ra2.at[m], ya_sem)
    sent += copies
    ra2[y] = a2s[...]
    for batch in PACE[1]:
        tail_start(batch)

    loads[5].wait()
    token = lax.broadcasted_iota(jnp.int32, (1, tokens), 1)
    page = lax.shift_right_logical(token, 4)
    for r in range(ROWS):
        inside = ctx * tokens + token < ctx_len[r]
        for s in range(STEPS):
            rel = sel_v[s, r] - ctx * pages_here
            bit = lax.shift_left(jnp.ones_like(rel), jnp.bitwise_and(rel, 15)).astype(jnp.float32)
            low = jnp.sum(jnp.where((rel >= 0) & (rel < 16), bit, 0.0), axis=1, keepdims=True).astype(jnp.int32)
            high = jnp.sum(jnp.where((rel >= 16) & (rel < 32), bit, 0.0), axis=1, keepdims=True).astype(jnp.int32)
            word = jnp.where(page < 16, low, high)
            live = jnp.bitwise_and(lax.shift_right_logical(word, jnp.bitwise_and(page, 15)), 1) == 1
            bias[pl.ds(r * STEPS + s, 1), :] = jnp.where(live & inside, 0.0, NEG)

    wait()
    total = functools.reduce(lambda a, b: a + b, [ra2[i] for i in range(ny)])
    rounded = total.astype(jnp.bfloat16)
    my_q = rounded[:QR]
    new_kv = rounded.astype(jnp.float32)[QR:QR + 2 * STEPS]
    qsend[...] = my_q
    wait, copies = exchange(2, NZ, z_peer, z, lambda p: qsend, lambda m: qbuf.at[q_rows(m)], zq_sem)
    sent += copies
    qbuf[q_rows(z), :] = my_q
    for batch in PACE[2]:
        tail_start(batch)

    tail_token = lax.broadcasted_iota(jnp.int32, (1, tail_tokens), 1)
    slot = lax.shift_right_logical(tail_token, 4) + ctx * out_here
    tail_row = jnp.zeros((1, tail_tokens), jnp.int32)
    end = 0
    for r in range(ROWS):
        end = end + tail_count[r]
        tail_row = tail_row + jnp.where(slot >= end, 1, 0)
    loads[6].wait()
    loads[7].wait()
    wait()

    q_all = qbuf[...]
    scores_t = nt(q_all, tk_v[pl.ds(0, out_here)].reshape(tail_tokens, HD)) * score_scale
    q_row = lax.shift_right_logical(lax.broadcasted_iota(jnp.int32, (ROWS * QR, tail_tokens), 0), 4)
    scores_t = jnp.where(q_row == tail_row, scores_t, NEG)
    peak_t = jnp.max(scores_t, axis=1, keepdims=True)
    scores_r, peaks = [], []
    for r in range(ROWS):
        masked = nt(q_all[r * QR:(r + 1) * QR], k_v[r]) * score_scale
        masked = jnp.concatenate([
            masked[s * GROUP:(s + 1) * GROUP] + bias[pl.ds(r * STEPS + s, 1), :] for s in range(STEPS)
        ], axis=0)
        scores_r.append(masked)
        peaks.append(jnp.maximum(jnp.max(masked, axis=1, keepdims=True), peak_t[r * QR:(r + 1) * QR]))
    weights_t = jnp.exp(scores_t - jnp.concatenate(peaks, axis=0))
    sums_t = jnp.sum(weights_t, axis=1, keepdims=True)
    out_t = nn(weights_t.astype(jnp.bfloat16), tv_v[pl.ds(0, out_here)].reshape(tail_tokens, HD))
    lane8 = lax.broadcasted_iota(jnp.int32, (8, HD), 1)

    def pack(m, l):
        return jnp.where(
            lane8 < 32, m[:8], jnp.where(lane8 < 64, m[8:], jnp.where(lane8 < 96, l[:8], l[8:]))
        )

    for r in range(ROWS):
        weights_r = jnp.exp(scores_r[r] - peaks[r])
        sums = jnp.sum(weights_r, axis=1, keepdims=True) + sums_t[r * QR:(r + 1) * QR]
        out_r = nn(weights_r.astype(jnp.bfloat16), v_v[r]) + out_t[r * QR:(r + 1) * QR]
        bsend[pl.ds(r * PIECE, QR), :] = out_r
        bsend[pl.ds(r * PIECE + QR, 8), :] = pack(peaks[r], sums)

    wait, copies = exchange(3, NZ, z_peer, z, lambda p: bsend.at[piece(p)], lambda m: rb1.at[m], zb_sem)
    sent += copies
    rb1[z] = bsend[piece(z), :]
    for batch in PACE[3]:
        tail_start(batch)

    q_f = my_q.astype(jnp.float32)
    own_scores = [
        jnp.sum(q_f * new_kv[u:u + 1], axis=1, keepdims=True) * score_scale for u in range(STEPS)
    ]
    step_of = lax.shift_right_logical(lax.broadcasted_iota(jnp.int32, (QR, 1), 0), 3)
    own_scores = [jnp.where(step_of >= u, own_scores[u], NEG) for u in range(STEPS)]

    def merge(ref, count):
        tiles = [ref[i, pl.ds(QR, 8), :] for i in range(count)]
        ms = [jnp.concatenate([t[:, 0:1], t[:, 32:33]], axis=0) for t in tiles]
        ls = [jnp.concatenate([t[:, 64:65], t[:, 96:97]], axis=0) for t in tiles]
        return ms, ls, [ref[i, pl.ds(0, QR), :] for i in range(count)]

    def combine(ms, ls, os):
        m = functools.reduce(jnp.maximum, ms)
        factors = [jnp.exp(a - m) for a in ms]
        l = functools.reduce(lambda a, b: a + b, [f * a for f, a in zip(factors, ls)])
        o = functools.reduce(lambda a, b: a + b, [f * a for f, a in zip(factors, os)])
        return m, l, o

    wait()
    m, l, o = combine(*merge(rb1, NZ))
    b2s[pl.ds(0, QR), :] = o
    b2s[pl.ds(QR, 8), :] = pack(m, l)
    wait, copies = exchange(4, ny, y_peer, y, lambda p: b2s, lambda m: rb2.at[m], yb_sem)
    sent += copies
    rb2[y] = b2s[...]
    wait()
    ms, ls, os = merge(rb2, ny)
    peak = functools.reduce(jnp.maximum, ms + own_scores)
    factors = [jnp.exp(a - peak) for a in ms]
    own = [jnp.exp(a - peak) for a in own_scores]
    l = functools.reduce(lambda a, b: a + b, [f * a for f, a in zip(factors, ls)] + own)
    o = functools.reduce(lambda a, b: a + b, [f * a for f, a in zip(factors, os)] + [
        w.astype(jnp.bfloat16).astype(jnp.float32) * new_kv[STEPS + u:STEPS + u + 1] for u, w in enumerate(own)
    ])
    att = (o / l).astype(jnp.bfloat16)
    asend[...] = att
    wait, copies = exchange(5, NZ, z_peer, z, lambda p: asend, lambda m: abuf.at[q_rows(m)], zt_sem)
    sent += copies
    abuf[q_rows(z), :] = att
    loads[8].wait()
    wait()
    attf[...] = abuf[...].astype(jnp.float32)
    att_all = jnp.concatenate([
        jnp.concatenate([attf[pl.ds(s * GROUP + g, ROWS, stride=QR), :] for s in range(STEPS)], axis=0)
        for g in range(GROUP)
    ], axis=1).astype(jnp.bfloat16)
    mine = nn(att_all, wo_v[...])
    csend[...] = mine
    wait, copies = exchange(6, nkv, kv_peer, kv, lambda p: csend, lambda m: rc.at[m], kv_sem)
    sent += copies
    rc[kv] = mine
    wait()
    mixed[...] = functools.reduce(lambda a, b: a + b, [rc[i] for i in range(nkv)]).astype(jnp.bfloat16)

    stores = []
    for batch, distance in enumerate(ORDER):
        from_z = lax.rem(z + NZ - distance, NZ)
        rows = pl.ds(from_z * ny, ny)
        pltpu.make_async_copy(trecv.at[rows], trecv.at[rows], tail_recv.at[from_z]).wait()
        for which, ref in enumerate((out_k, out_v)):
            store = pltpu.make_async_copy(trecv.at[rows, which], ref.at[rows], out_sem.at[batch, which])
            store.start()
            stores.append(store)
        pages = trecv[rows, 0].astype(jnp.float32).reshape(ny * PAIR, PAGE, HD)
        at = pl.ds(pl.multiple_of(from_z * (ny * PAIR), ny * PAIR), ny * PAIR)
        out_min[at, :] = jnp.min(pages, axis=1).astype(jnp.bfloat16)
        out_max[at, :] = jnp.max(pages, axis=1).astype(jnp.bfloat16)
    for store in stores:
        store.wait()
    for copy in sent:
        copy.wait_send()
    for distance in range(NZ):
        sent_rows = pl.ds(0, ny - 1 if distance == 0 else ny)
        if ny > 1 or distance > 0:
            pltpu.make_async_copy(stage.at[sent_rows], stage.at[sent_rows], tail_send.at[distance]).wait()


def on_device(
    hidden, w_qkv, w_out, key_pages, value_pages, ctx_len, selected,
    tail_keys, tail_values, tail_count, tail_dest,
):
    n_ctx = lax.axis_size("ctx")
    nkv = lax.axis_size("kv")
    ny = n_ctx // NZ
    pages_here = key_pages.shape[1]
    out_here = tail_keys.shape[0]
    tokens = pages_here * PAGE
    tail_tokens = out_here * PAGE
    bf, f32, i32 = jnp.bfloat16, jnp.float32, jnp.int32
    any_spec = pl.BlockSpec(memory_space=pl.ANY)
    smem = pl.BlockSpec(memory_space=pltpu.SMEM)
    vmem = pl.BlockSpec(memory_space=pltpu.VMEM)
    dma = pltpu.SemaphoreType.DMA
    mixed, out_k, out_v, low, high = pl.pallas_call(
        functools.partial(body, ny, nkv, out_here, pages_here),
        out_shape=(
            jax.ShapeDtypeStruct((STEPS * ROWS, HD), bf),
            jax.ShapeDtypeStruct((n_ctx, PAIR, PAGE, HD), bf),
            jax.ShapeDtypeStruct((n_ctx, PAIR, PAGE, HD), bf),
            jax.ShapeDtypeStruct((n_ctx * PAIR, HD), bf),
            jax.ShapeDtypeStruct((n_ctx * PAIR, HD), bf),
        ),
        in_specs=[smem, smem] + [any_spec] * 9,
        out_specs=(vmem, any_spec, any_spec, vmem, vmem),
        scratch_shapes=[
            pltpu.VMEM((STEPS * ROWS, HD), bf),
            pltpu.VMEM(w_qkv.shape, bf),
            pltpu.VMEM(w_out.shape, bf),
            pltpu.VMEM((ROWS, tokens, HD), bf),
            pltpu.VMEM((ROWS, tokens, HD), bf),
            pltpu.VMEM(selected.shape, i32),
            pltpu.VMEM((1, 128), i32),
            pltpu.VMEM((out_here + 1, PAGE, HD), bf),
            pltpu.VMEM((out_here + 1, PAGE, HD), bf),
            pltpu.VMEM((ROWS * PIECE, HD), f32),
            pltpu.VMEM((NZ, PIECE, HD), f32),
            pltpu.VMEM((PIECE, HD), f32),
            pltpu.VMEM((ny, PIECE, HD), f32),
            pltpu.VMEM((QR, HD), bf),
            pltpu.VMEM((ROWS * QR, HD), bf),
            pltpu.VMEM((ROWS * STEPS, tokens), f32),
            pltpu.VMEM((ROWS * PIECE, HD), f32),
            pltpu.VMEM((NZ, PIECE, HD), f32),
            pltpu.VMEM((PIECE, HD), f32),
            pltpu.VMEM((ny, PIECE, HD), f32),
            pltpu.VMEM((QR, HD), bf),
            pltpu.VMEM((ROWS * QR, HD), bf),
            pltpu.VMEM((ROWS * QR, HD), f32),
            pltpu.VMEM((STEPS * ROWS, HD), f32),
            pltpu.VMEM((nkv, STEPS * ROWS, HD), f32),
            pltpu.VMEM((n_ctx, 2, PAIR, PAGE, HD), bf),
            pltpu.VMEM((n_ctx, 2, PAIR, PAGE, HD), bf),
            pltpu.VMEM((8, 128), i32),
            pltpu.SMEM((8, 128), i32),
            dma((9,)),
            dma((7, 8)),
            dma((NZ,)),
            dma((ny,)),
            dma((NZ,)),
            dma((NZ,)),
            dma((ny,)),
            dma((NZ,)),
            dma((nkv,)),
            dma((NZ,)),
            dma((NZ,)),
            dma((NZ, 2)),
            dma((1,)),
            pltpu.SemaphoreType.REGULAR,
        ],
        compiler_params=pltpu.CompilerParams(
            collective_id=0, has_side_effects=True, vmem_limit_bytes=32 * 1024 * 1024
        ),
    )(
        ctx_len, tail_count, hidden.reshape(STEPS * ROWS, HD), w_qkv, w_out,
        key_pages.reshape(ROWS, tokens, HD), value_pages.reshape(ROWS, tokens, HD), selected,
        tail_keys, tail_values, tail_dest.T,
    )
    return (
        mixed.reshape(STEPS, ROWS, HD),
        out_k.reshape(n_ctx * PAIR, PAGE, HD),
        out_v.reshape(n_ctx * PAIR, PAGE, HD),
        jnp.stack([low, high], axis=1),
    )


def solution(mesh):
    placed = (
        P(None, None, "ctx"),
        P("ctx", "kv"),
        P("kv", "ctx"),
        P(None, "ctx", None, "kv"),
        P(None, "ctx", None, "kv"),
        P(),
        P(None, None, "kv", None),
        P("ctx", None, "kv"),
        P("ctx", None, "kv"),
        P(),
        P(),
    )
    return jax.shard_map(
        on_device,
        mesh=mesh,
        in_specs=placed,
        out_specs=(
            P(None, None, "ctx"),
            P("ctx", None, "kv"),
            P("ctx", None, "kv"),
            P("ctx", None, "kv"),
        ),
        check_vma=False,
    )
```

time: 807 us -> 83.2 us (0.10)
  blocking collectives: 474 us -> 0 us
  waiting for transfers between devices: 264 us -> 0 us
  Pallas kernels: 0 us -> 70.8 us
  starting transfers between devices: 26.9 us -> 0 us
  between operations: 14.5 us -> 0.69 us
  matrix products: 10.4 us -> 0 us
    psum x3 -> x0, blocking collectives: 354 us -> none  [the longest x1 224 us: on_device(): projected = lax.psum(partial_qkv, 'ctx')]
    psum x1 -> x0, waiting for transfers between devices: 251 us -> none  [on_device(): lax.psum((resident_totals + tail_totals, resident_weighted + tail_weighte...]
    pmax x1 -> x0, blocking collectives: 119 us -> none  [on_device(): lax.pmax(local_peak, 'ctx')]
    pallas_call x0 -> x1, Pallas kernels: none -> 70.8 us  [on_device(): pl.pallas_call(functools.partial(body, ny, nkv, out_here, pages_here), ou...]
    all_to_all x3 -> x0, starting transfers between devices: 26.9 us -> none  [the longest x1 17.1 us: on_device(): lax.all_to_all(send_bounds, 'ctx', split_axis=0, concat_axis=0, tiled=True)]
    all_to_all x3 -> x0, waiting for transfers between devices: 12.6 us -> none  [the longest x1 12.6 us: on_device(): lax.all_to_all(send_keys, 'ctx', split_axis=0, concat_axis=0, tiled=True)]
    dot_general x13 -> x0, matrix products: 10.4 us -> none  [the longest x1 2.57 us: page_scores(): jnp.einsum('sphgd,pthd->sphgt', page_query, keys_four, preferred_element_...]
  transfers between devices with their start and end apart: 4 -> 0, of which waited for: 2 -> 0; matrix products, arithmetic and copies ran while one was open for 2% -> 0% of each run, Pallas kernels for 0% -> 0%
where the time goes in v1:
time: 83.2 us; the launch traced here: 82.7 us
  Pallas kernels  70.8 us (85%)
  local copies, waits for them, and re-layouts  11.2 us (13%)
    pallas_call x1, Pallas kernels, on_device(): pl.pallas_call(functools.partial(body, ny, nkv, out_here, pages_here), ou...  70.8 us
    unnamed x26, local copies, waits for them, and re-layouts  11.2 us

profile of v1, /device:TPU:1, one launch (start us, length us, event | category | flops | bytes accessed | tf_op | source)
XLA Modules:
  0.0 82.7 jit_solution(11756912159827682695)
XLA Ops:
  0.6 0.0 copy-start.8
  0.6 0.0 copy-start.9
  0.7 0.0 copy-start.10
  0.7 0.7 copy-done.8
  1.3 0.0 copy-done.9
  1.3 0.0 copy-done.10
  1.3 0.0 copy-start
  1.3 1.2 %copy-done = bf16[8,32,16,128]{3,2,1,0:T(8,128)(2,1)S(1)} copy-done((bf16[8,32,16,128]{3,2,1,0:T(8,128)(2,1)S(1)}, bf16[8,32,16,128]{3,2,1,0:T(8,128)(2,1)}, u32[]{:S(2)}) %copy-start) | copy-done | bytes 1048600
  2.6 0.0 copy-start.1
  2.6 1.2 %copy-done.1 = bf16[8,32,16,128]{3,2,1,0:T(8,128)(2,1)S(1)} copy-done((bf16[8,32,16,128]{3,2,1,0:T(8,128)(2,1)S(1)}, bf16[8,32,16,128]{3,2,1,0:T(8,128)(2,1)}, u32[]{:S(2)}) %copy-start.1) | copy-done | bytes 1048600
  3.8 0.0 copy-start.2
  3.8 1.0 %copy-done.2 = bf16[128,1280]{1,0:T(8,128)(2,1)S(1)} copy-done((bf16[128,1280]{1,0:T(8,128)(2,1)S(1)}, bf16[128,1280]{1,0:T(8,128)(2,1)}, u32[]{:S(2)}) %copy-start.2) | copy-done | bytes 327704
  4.8 0.0 copy-start.3
  4.8 0.9 %copy-done.3 = bf16[1024,128]{1,0:T(8,128)(2,1)S(1)} copy-done((bf16[1024,128]{1,0:T(8,128)(2,1)S(1)}, bf16[1024,128]{1,0:T(8,128)(2,1)}, u32[]{:S(2)}) %copy-start.3) | copy-done | bytes 262168
  5.7 0.0 copy-start.4
  5.7 0.9 %copy-done.4 = bf16[64,16,128]{2,1,0:T(8,128)(2,1)S(1)} copy-done((bf16[64,16,128]{2,1,0:T(8,128)(2,1)S(1)}, bf16[64,16,128]{2,1,0:T(8,128)(2,1)}, u32[]{:S(2)}) %copy-start.4) | copy-done | bytes 262168
  6.7 0.0 copy-start.5
  6.7 0.9 %copy-done.5 = bf16[64,16,128]{2,1,0:T(8,128)(2,1)S(1)} copy-done((bf16[64,16,128]{2,1,0:T(8,128)(2,1)S(1)}, bf16[64,16,128]{2,1,0:T(8,128)(2,1)}, u32[]{:S(2)}) %copy-start.5) | copy-done | bytes 262168
  7.6 0.0 copy-start.6
  7.6 0.7 copy-done.6
  8.3 0.0 copy-start.7
  8.3 0.7 copy-done.7
  9.0 70.8 %shard_map.138 = (bf16[16,128]{1,0:T(8,128)(2,1)S(1)}, bf16[64,2,16,128]{3,2,1,0:T(8,128)(2,1)S(1)}, bf16[64,2,16,128]{3,2,1,0:T(8,128)(2,1)S(1)}, bf16[128,128]{1,0:T(8,128)(2,1)S(1)}, bf16[128,128]{1,0:T(8,128)(2,1)S(1)}) custom-call(s32[8]{0:T(128)S(1)} %copy-done.9, s32[8]{0:T(128)S(1)} %copy-done.10, bf16[16,128]{1,0:T(8,128)(2,1)S(1)} %bitcast.16, ...), custom_call_target="tpu_custom_call" | custom-call | tf_op jit(solution)/shard_map/pallas_call | solution.py:364
  79.8 0.7 copy.15
  80.5 0.6 copy.19
  81.1 0.8 copy.20
  81.9 0.8 copy.21
  (1 shorter events, 0.0 us)
Async XLA Ops:
  0.6 0.7 copy-start.8
  0.6 0.7 copy-start.9
  0.7 0.7 copy-start.10
  1.3 1.2 %copy-start = (bf16[8,32,16,128]{3,2,1,0:T(8,128)(2,1)S(1)}, bf16[8,32,16,128]{3,2,1,0:T(8,128)(2,1)}, u32[]{:S(2)}) copy-start(bf16[8,32,16,128]{3,2,1,0:T(8,128)(2,1)} %param.14) | copy-start | bytes 3145732
  2.6 1.2 %copy-start.1 = (bf16[8,32,16,128]{3,2,1,0:T(8,128)(2,1)S(1)}, bf16[8,32,16,128]{3,2,1,0:T(8,128)(2,1)}, u32[]{:S(2)}) copy-start(bf16[8,32,16,128]{3,2,1,0:T(8,128)(2,1)} %param.15) | copy-start | bytes 3145732
  3.8 1.0 %copy-start.2 = (bf16[128,1280]{1,0:T(8,128)(2,1)S(1)}, bf16[128,1280]{1,0:T(8,128)(2,1)}, u32[]{:S(2)}) copy-start(bf16[128,1280]{1,0:T(8,128)(2,1)} %w_qkv.1) | copy-start | bytes 983044
  4.8 0.9 %copy-start.3 = (bf16[1024,128]{1,0:T(8,128)(2,1)S(1)}, bf16[1024,128]{1,0:T(8,128)(2,1)}, u32[]{:S(2)}) copy-start(bf16[1024,128]{1,0:T(8,128)(2,1)} %w_out.1) | copy-start | bytes 786436
  5.7 0.9 %copy-start.4 = (bf16[64,16,128]{2,1,0:T(8,128)(2,1)S(1)}, bf16[64,16,128]{2,1,0:T(8,128)(2,1)}, u32[]{:S(2)}) copy-start(bf16[64,16,128]{2,1,0:T(8,128)(2,1)} %tail_k.1) | copy-start | bytes 786436
  6.7 0.9 %copy-start.5 = (bf16[64,16,128]{2,1,0:T(8,128)(2,1)S(1)}, bf16[64,16,128]{2,1,0:T(8,128)(2,1)}, u32[]{:S(2)}) copy-start(bf16[64,16,128]{2,1,0:T(8,128)(2,1)} %tail_v.1) | copy-start | bytes 786436
  7.6 0.7 copy-start.6
  8.3 0.7 copy-start.7

commit v2 on v1

--- a/solution.py
+++ b/solution.py
@@ -19,8 +19,11 @@
 PIECE = 24
 NEG = -1e30
 MESH = pl.DeviceIdType.MESH
-ORDER = (1, 7, 2, 6, 3, 5, 4, 0)
-PACE = ((0, 1), (2, 3), (4, 5), (6, 7))
+SCHEDULE = (((0, 2),), ((1, 2),), ((0, 5),), ((1, 5),), ((3, 2),), ((2, 3),), ((2, 4), (3, 5)))
+
+
+def far_first(count):
+    return sorted(range(1, count), key=lambda d: (-min(d, count - d), d))
 
 
 def nt(a, b):
@@ -34,12 +37,12 @@
 def body(
     ny, nkv, out_here, pages_here,
     ctx_len, tail_count, hidden, w_qkv, w_out, keys, values, selected, tail_k, tail_v, dest,
-    mixed, out_k, out_v, out_min, out_max,
+    mixed, got_k, got_v,
     hid_v, wq_v, wo_v, k_v, v_v, sel_v, dest_v, tk_v, tv_v,
     part, ra1, a2s, ra2, qsend, qbuf, bias, bsend, rb1, b2s, rb2, asend, abuf, attf, csend, rc,
-    stage, trecv, inv_v, inv_s,
-    in_sem, send_sem, za_sem, ya_sem, zq_sem, zb_sem, yb_sem, zt_sem, kv_sem,
-    tail_send, tail_recv, out_sem, inv_sem, ready,
+    stage_k, stage_v, mid_k, mid_v, inv_v, inv_s,
+    in_sem, send_sem, za_sem, ya_sem, zq_sem, yb_sem, zb_sem, yt_sem, kv_sem,
+    tail_send, tail_recv, inv_sem,
 ):
     ctx = lax.axis_index("ctx")
     kv = lax.axis_index("kv")
@@ -112,8 +115,6 @@
             part[pl.ds(at, ROWS, stride=PIECE), :] = proj[s * ROWS:(s + 1) * ROWS, j * HD:(j + 1) * HD]
 
     pl.semaphore_wait(barrier, peers)
-    for d in range(1, ny):
-        pl.semaphore_signal(ready, inc=1, device_id=y_peer(d)[1], device_id_type=MESH)
 
     def piece(i):
         return pl.ds(pl.multiple_of(i * PIECE, 8), PIECE)
@@ -144,25 +145,29 @@
 
     sent = []
 
-    def tail_block(distance, i):
-        to_z = lax.rem(z + distance, NZ)
-        to_y = lax.rem(y + i, ny)
-        return pltpu.make_async_remote_copy(
-            src_ref=stage.at[to_z * ny + to_y], dst_ref=trecv.at[ctx],
-            send_sem=tail_send.at[distance], recv_sem=tail_recv.at[z],
-            device_id=(to_z * ny + to_y, kv), device_id_type=MESH,
-        )
-
-    def tail_start(batch):
-        distance = ORDER[batch]
-        if distance == 0:
-            pltpu.make_async_copy(stage.at[ctx], trecv.at[ctx], tail_recv.at[z]).start()
-
-        def start(i, carry):
-            tail_block(distance, i).start()
-            return carry
-
-        lax.fori_loop(1 if distance == 0 else 0, ny, start, 0)
+    tail_peer = (y_peer, z_peer, z_peer, y_peer)
+    tail_order = (far_first(ny), far_first(NZ), far_first(NZ), far_first(ny))
+    tail_src = (
+        lambda p: stage_k.at[p], lambda p: stage_v.at[p], lambda p: mid_k.at[:, p], lambda p: mid_v.at[:, p],
+    )
+    tail_dst = (mid_k.at[y], mid_v.at[z], got_k.at[z], got_v.at[:, y])
+    tail_me = (y, z, z, y)
+    landing = (mid_k, mid_v, got_k, got_v)
+    begun = [0, 0, 0, 0]
+
+    def tail_start(phase):
+        for kind, number in SCHEDULE[phase]:
+            if begun[kind] == 0:
+                if kind >= 2:
+                    pltpu.make_async_copy(landing[kind - 2], landing[kind - 2], tail_recv.at[kind - 2]).wait()
+                pltpu.make_async_copy(tail_src[kind](tail_me[kind]), tail_dst[kind], tail_recv.at[kind]).start()
+            for d in tail_order[kind][begun[kind]:begun[kind] + number]:
+                peer, device = tail_peer[kind](d)
+                pltpu.make_async_remote_copy(
+                    src_ref=tail_src[kind](peer), dst_ref=tail_dst[kind], send_sem=tail_send.at[kind],
+                    recv_sem=tail_recv.at[kind], device_id=device, device_id_type=MESH,
+                ).start()
+            begun[kind] += number
 
     wait, copies = exchange(0, NZ, z_peer, z, lambda p: part.at[piece(p)], lambda m: ra1.at[m], za_sem)
     sent += copies
@@ -173,25 +178,23 @@
     table_copy.wait()
 
     def place(d, carry):
+        to_z = lax.div(d, ny)
+        to_y = lax.rem(d, ny)
         for k in range(PAIR):
             page = inv_s[0, d * PAIR + k]
-            stage[d, 0, k] = tk_v[page]
-            stage[d, 1, k] = tv_v[page]
+            stage_k[to_y, to_z, k] = tk_v[page]
+            stage_v[to_z, to_y, k] = tv_v[page]
         return carry
 
     lax.fori_loop(0, n_ctx, place, 0)
-    if ny > 1:
-        pl.semaphore_wait(ready, ny - 1)
-    for batch in PACE[0]:
-        tail_start(batch)
+    tail_start(0)
 
     wait()
     a2s[...] = functools.reduce(lambda a, b: a + b, [ra1[i] for i in range(NZ)])
     wait, copies = exchange(1, ny, y_peer, y, lambda p: a2s, lambda m: ra2.at[m], ya_sem)
     sent += copies
     ra2[y] = a2s[...]
-    for batch in PACE[1]:
-        tail_start(batch)
+    tail_start(1)
 
     loads[5].wait()
     token = lax.broadcasted_iota(jnp.int32, (1, tokens), 1)
@@ -216,8 +219,7 @@
     wait, copies = exchange(2, NZ, z_peer, z, lambda p: qsend, lambda m: qbuf.at[q_rows(m)], zq_sem)
     sent += copies
     qbuf[q_rows(z), :] = my_q
-    for batch in PACE[2]:
-        tail_start(batch)
+    tail_start(2)
 
     tail_token = lax.broadcasted_iota(jnp.int32, (1, tail_tokens), 1)
     slot = lax.shift_right_logical(tail_token, 4) + ctx * out_here
@@ -260,18 +262,17 @@
         bsend[pl.ds(r * PIECE, QR), :] = out_r
         bsend[pl.ds(r * PIECE + QR, 8), :] = pack(peaks[r], sums)
 
-    wait, copies = exchange(3, NZ, z_peer, z, lambda p: bsend.at[piece(p)], lambda m: rb1.at[m], zb_sem)
-    sent += copies
-    rb1[z] = bsend[piece(z), :]
-    for batch in PACE[3]:
-        tail_start(batch)
+    wait, copies = exchange(3, ny, y_peer, y, lambda p: bsend.at[piece(p)], lambda m: rb1.at[m], yb_sem)
+    sent += copies
+    rb1[y] = bsend[piece(y), :]
+    tail_start(3)
 
     q_f = my_q.astype(jnp.float32)
     own_scores = [
         jnp.sum(q_f * new_kv[u:u + 1], axis=1, keepdims=True) * score_scale for u in range(STEPS)
     ]
     step_of = lax.shift_right_logical(lax.broadcasted_iota(jnp.int32, (QR, 1), 0), 3)
-    own_scores = [jnp.where(step_of >= u, own_scores[u], NEG) for u in range(STEPS)]
+    own_scores = [jnp.where((step_of >= u) & (z == y), own_scores[u], NEG) for u in range(STEPS)]
 
     def merge(ref, count):
         tiles = [ref[i, pl.ds(QR, 8), :] for i in range(count)]
@@ -279,34 +280,35 @@
         ls = [jnp.concatenate([t[:, 64:65], t[:, 96:97]], axis=0) for t in tiles]
         return ms, ls, [ref[i, pl.ds(0, QR), :] for i in range(count)]
 
-    def combine(ms, ls, os):
-        m = functools.reduce(jnp.maximum, ms)
+    def combine(ms, ls, os, m):
         factors = [jnp.exp(a - m) for a in ms]
         l = functools.reduce(lambda a, b: a + b, [f * a for f, a in zip(factors, ls)])
         o = functools.reduce(lambda a, b: a + b, [f * a for f, a in zip(factors, os)])
         return m, l, o
 
     wait()
-    m, l, o = combine(*merge(rb1, NZ))
+    ms, ls, os = merge(rb1, ny)
+    peak = functools.reduce(jnp.maximum, ms + own_scores)
+    own = [jnp.exp(a - peak) for a in own_scores]
+    _, l, o = combine(ms, ls, os, peak)
+    for u, w in enumerate(own):
+        l = l + w
+        o = o + w.astype(jnp.bfloat16).astype(jnp.float32) * new_kv[STEPS + u:STEPS + u + 1]
     b2s[pl.ds(0, QR), :] = o
-    b2s[pl.ds(QR, 8), :] = pack(m, l)
-    wait, copies = exchange(4, ny, y_peer, y, lambda p: b2s, lambda m: rb2.at[m], yb_sem)
-    sent += copies
-    rb2[y] = b2s[...]
-    wait()
-    ms, ls, os = merge(rb2, ny)
-    peak = functools.reduce(jnp.maximum, ms + own_scores)
-    factors = [jnp.exp(a - peak) for a in ms]
-    own = [jnp.exp(a - peak) for a in own_scores]
-    l = functools.reduce(lambda a, b: a + b, [f * a for f, a in zip(factors, ls)] + own)
-    o = functools.reduce(lambda a, b: a + b, [f * a for f, a in zip(factors, os)] + [
-        w.astype(jnp.bfloat16).astype(jnp.float32) * new_kv[STEPS + u:STEPS + u + 1] for u, w in enumerate(own)
-    ])
+    b2s[pl.ds(QR, 8), :] = pack(peak, l)
+    wait, copies = exchange(4, NZ, z_peer, z, lambda p: b2s, lambda m: rb2.at[m], zb_sem)
+    sent += copies
+    rb2[z] = b2s[...]
+    tail_start(4)
+    wait()
+    ms, ls, os = merge(rb2, NZ)
+    _, l, o = combine(ms, ls, os, functools.reduce(jnp.maximum, ms))
     att = (o / l).astype(jnp.bfloat16)
     asend[...] = att
-    wait, copies = exchange(5, NZ, z_peer, z, lambda p: asend, lambda m: abuf.at[q_rows(m)], zt_sem)
-    sent += copies
-    abuf[q_rows(z), :] = att
+    wait, copies = exchange(5, ny, y_peer, y, lambda p: asend, lambda m: abuf.at[q_rows(m)], yt_sem)
+    sent += copies
+    abuf[q_rows(y), :] = att
+    tail_start(5)
     loads[8].wait()
     wait()
     attf[...] = abuf[...].astype(jnp.float32)
@@ -319,30 +321,37 @@
     wait, copies = exchange(6, nkv, kv_peer, kv, lambda p: csend, lambda m: rc.at[m], kv_sem)
     sent += copies
     rc[kv] = mine
+    tail_start(6)
     wait()
     mixed[...] = functools.reduce(lambda a, b: a + b, [rc[i] for i in range(nkv)]).astype(jnp.bfloat16)
 
-    stores = []
-    for batch, distance in enumerate(ORDER):
-        from_z = lax.rem(z + NZ - distance, NZ)
-        rows = pl.ds(from_z * ny, ny)
-        pltpu.make_async_copy(trecv.at[rows], trecv.at[rows], tail_recv.at[from_z]).wait()
-        for which, ref in enumerate((out_k, out_v)):
-            store = pltpu.make_async_copy(trecv.at[rows, which], ref.at[rows], out_sem.at[batch, which])
-            store.start()
-            stores.append(store)
-        pages = trecv[rows, 0].astype(jnp.float32).reshape(ny * PAIR, PAGE, HD)
-        at = pl.ds(pl.multiple_of(from_z * (ny * PAIR), ny * PAIR), ny * PAIR)
-        out_min[at, :] = jnp.min(pages, axis=1).astype(jnp.bfloat16)
-        out_max[at, :] = jnp.max(pages, axis=1).astype(jnp.bfloat16)
-    for store in stores:
-        store.wait()
     for copy in sent:
         copy.wait_send()
-    for distance in range(NZ):
-        sent_rows = pl.ds(0, ny - 1 if distance == 0 else ny)
-        if ny > 1 or distance > 0:
-            pltpu.make_async_copy(stage.at[sent_rows], stage.at[sent_rows], tail_send.at[distance]).wait()
+    for kind in (2, 3):
+        pltpu.make_async_copy(landing[kind], landing[kind], tail_recv.at[kind]).wait()
+    for kind, ref in enumerate((stage_k, stage_v, got_k, got_v)):
+        others = ref.at[pl.ds(0, len(tail_order[kind]))]
+        pltpu.make_async_copy(others, others, tail_send.at[kind]).wait()
+
+
+def store_body(nz, rows, got_k, got_v, mixed, out_k, out_v, bounds, sem):
+    mixed[...] = rows[...]
+    copies = [
+        pltpu.make_async_copy(got, out, sem.at[i]) for i, (got, out) in enumerate(((got_k, out_k), (got_v, out_v)))
+    ]
+    for copy in copies:
+        copy.start()
+    count = got_k.shape[1] * PAIR
+
+    def step(i, carry):
+        pages = got_k[i].astype(jnp.float32).reshape(count, PAGE, HD)
+        at = pl.ds(pl.multiple_of(i * count, count), count)
+        bounds[at] = jnp.stack([jnp.min(pages, axis=1), jnp.max(pages, axis=1)], axis=1).astype(jnp.bfloat16)
+        return carry
+
+    lax.fori_loop(0, nz, step, 0)
+    for copy in copies:
+        copy.wait()
 
 
 def on_device(
@@ -357,21 +366,21 @@
     tokens = pages_here * PAGE
     tail_tokens = out_here * PAGE
     bf, f32, i32 = jnp.bfloat16, jnp.float32, jnp.int32
-    any_spec = pl.BlockSpec(memory_space=pl.ANY)
+    any_spec = pl.BlockSpec(memory_space=pltpu.HBM)
     smem = pl.BlockSpec(memory_space=pltpu.SMEM)
     vmem = pl.BlockSpec(memory_space=pltpu.VMEM)
     dma = pltpu.SemaphoreType.DMA
-    mixed, out_k, out_v, low, high = pl.pallas_call(
+    tail_shape = (NZ, ny, PAIR, PAGE, HD)
+    turned = (ny, NZ, PAIR, PAGE, HD)
+    rows, got_k, got_v = pl.pallas_call(
         functools.partial(body, ny, nkv, out_here, pages_here),
         out_shape=(
-            jax.ShapeDtypeStruct((STEPS * ROWS, HD), bf),
-            jax.ShapeDtypeStruct((n_ctx, PAIR, PAGE, HD), bf),
-            jax.ShapeDtypeStruct((n_ctx, PAIR, PAGE, HD), bf),
-            jax.ShapeDtypeStruct((n_ctx * PAIR, HD), bf),
-            jax.ShapeDtypeStruct((n_ctx * PAIR, HD), bf),
+            pltpu.VMEM((STEPS * ROWS, HD), bf),
+            pltpu.VMEM(tail_shape, bf),
+            pltpu.VMEM(tail_shape, bf),
         ),
         in_specs=[smem, smem] + [any_spec] * 9,
-        out_specs=(vmem, any_spec, any_spec, vmem, vmem),
+        out_specs=(vmem, vmem, vmem),
         scratch_shapes=[
             pltpu.VMEM((STEPS * ROWS, HD), bf),
             pltpu.VMEM(w_qkv.shape, bf),
@@ -390,16 +399,18 @@
             pltpu.VMEM((ROWS * QR, HD), bf),
             pltpu.VMEM((ROWS * STEPS, tokens), f32),
             pltpu.VMEM((ROWS * PIECE, HD), f32),
+            pltpu.VMEM((ny, PIECE, HD), f32),
+            pltpu.VMEM((PIECE, HD), f32),
             pltpu.VMEM((NZ, PIECE, HD), f32),
-            pltpu.VMEM((PIECE, HD), f32),
-            pltpu.VMEM((ny, PIECE, HD), f32),
             pltpu.VMEM((QR, HD), bf),
             pltpu.VMEM((ROWS * QR, HD), bf),
             pltpu.VMEM((ROWS * QR, HD), f32),
             pltpu.VMEM((STEPS * ROWS, HD), f32),
             pltpu.VMEM((nkv, STEPS * ROWS, HD), f32),
-            pltpu.VMEM((n_ctx, 2, PAIR, PAGE, HD), bf),
-            pltpu.VMEM((n_ctx, 2, PAIR, PAGE, HD), bf),
+            pltpu.VMEM(turned, bf),
+            pltpu.VMEM(tail_shape, bf),
+            pltpu.VMEM(turned, bf),
+            pltpu.VMEM(tail_shape, bf),
             pltpu.VMEM((8, 128), i32),
             pltpu.SMEM((8, 128), i32),
             dma((9,)),
@@ -407,29 +418,40 @@
             dma((NZ,)),
             dma((ny,)),
             dma((NZ,)),
+            dma((ny,)),
             dma((NZ,)),
             dma((ny,)),
-            dma((NZ,)),
             dma((nkv,)),
-            dma((NZ,)),
-            dma((NZ,)),
-            dma((NZ, 2)),
+            dma((4,)),
+            dma((4,)),
             dma((1,)),
-            pltpu.SemaphoreType.REGULAR,
         ],
         compiler_params=pltpu.CompilerParams(
-            collective_id=0, has_side_effects=True, vmem_limit_bytes=32 * 1024 * 1024
+            collective_id=0, has_side_effects=True, vmem_limit_bytes=60 * 1024 * 1024
         ),
     )(
         ctx_len, tail_count, hidden.reshape(STEPS * ROWS, HD), w_qkv, w_out,
         key_pages.reshape(ROWS, tokens, HD), value_pages.reshape(ROWS, tokens, HD), selected,
         tail_keys, tail_values, tail_dest.T,
     )
+    mixed, out_k, out_v, bounds = pl.pallas_call(
+        functools.partial(store_body, NZ),
+        out_shape=(
+            jax.ShapeDtypeStruct((STEPS * ROWS, HD), bf),
+            jax.ShapeDtypeStruct(tail_shape, bf),
+            jax.ShapeDtypeStruct(tail_shape, bf),
+            jax.ShapeDtypeStruct((n_ctx * PAIR, 2, HD), bf),
+        ),
+        in_specs=[vmem, vmem, vmem],
+        out_specs=(vmem, any_spec, any_spec, vmem),
+        scratch_shapes=[dma((2,))],
+        compiler_params=pltpu.CompilerParams(vmem_limit_bytes=16 * 1024 * 1024),
+    )(rows, got_k, got_v)
     return (
         mixed.reshape(STEPS, ROWS, HD),
         out_k.reshape(n_ctx * PAIR, PAGE, HD),
         out_v.reshape(n_ctx * PAIR, PAGE, HD),
-        jnp.stack([low, high], axis=1),
+        bounds,
     )
 
 

time: 83.2 us -> 63.3 us (0.76)
  local copies, waits for them, and re-layouts: 11.2 us -> 0 us
  Pallas kernels: 70.8 us -> 62.5 us
    unnamed x26 -> x0, local copies, waits for them, and re-layouts: 11.2 us -> none
    pallas_call x1, Pallas kernels: 70.8 us -> 60.9 us  [on_device(): pl.pallas_call(functools.partial(body, ny, nkv, out_here, pages_here), ou...]
    pallas_call x0 -> x1, Pallas kernels: none -> 1.62 us  [on_device(): pl.pallas_call(functools.partial(store_body, NZ), out_shape=(jax.ShapeDty...]
where the time goes in v2:
time: 63.3 us; the launch traced here: 63.2 us
  Pallas kernels  62.5 us (99%)
  between operations  0.64 us (1%)
    pallas_call x1, Pallas kernels, on_device(): pl.pallas_call(functools.partial(body, ny, nkv, out_here, pages_here), ou...  60.9 us
    pallas_call x1, Pallas kernels, on_device(): pl.pallas_call(functools.partial(store_body, NZ), out_shape=(jax.ShapeDty...  1.62 us

profile of v2, /device:TPU:1, one launch (start us, length us, event | category | flops | bytes accessed | tf_op | source)
XLA Modules:
  0.0 63.2 jit_solution(849492322349719520)
XLA Ops:
  0.6 60.9 %shard_map.138 = (bf16[16,128]{1,0:T(8,128)(2,1)S(1)}, bf16[8,8,2,16,128]{4,3,2,1,0:T(8,128)(2,1)S(1)}, bf16[8,8,2,16,128]{4,3,2,1,0:T(8,128)(2,1)S(1)}) custom-call(s32[8]{0:T(128)} %ctx_len.1, s32[8]{0:T(128)} %tail_count.1, bf16[16,128]{1,0:T(8,128)(2,1)} %bitcast.10, bf16[128,1280]{1,0:T(8,128)(2,1)} %w_qkv.1, bf16[1024,128]{1,0:T(8,128)(2,1)} %w_out.1, ...), custom_call_target="tpu_custom_call" | custom-call | tf_op jit(solution)/shard_map/pallas_call | solution.py:375
  61.6 1.6 %shard_map.139 = (bf16[16,128]{1,0:T(8,128)(2,1)}, bf16[8,8,2,16,128]{4,3,2,1,0:T(8,128)(2,1)}, bf16[8,8,2,16,128]{4,3,2,1,0:T(8,128)(2,1)}, bf16[128,2,128]{2,1,0:T(2,128)(2,1)}) custom-call(bf16[16,128]{1,0:T(8,128)(2,1)S(1)} %get-tuple-element.11.rows, bf16[8,8,2,16,128]{4,3,2,1,0:T(8,128)(2,1)S(1)} %get-tuple-element.12.got_k, ...), custom_call_target="tpu_custom_call" | custom-call | tf_op jit(solution)/shard_map/pallas_call | solution.py:437

commit v3 on v2

--- a/solution.py
+++ b/solution.py
@@ -19,7 +19,7 @@
 PIECE = 24
 NEG = -1e30
 MESH = pl.DeviceIdType.MESH
-SCHEDULE = (((0, 2),), ((1, 2),), ((0, 5),), ((1, 5),), ((3, 2),), ((2, 3),), ((2, 4), (3, 5)))
+SCHEDULE = (((0, 3),), ((1, 3),), ((0, 4),), ((1, 4),), ((3, 3),), ((2, 3),), ((2, 4), (3, 4)), ())
 
 
 def far_first(count):
@@ -68,7 +68,7 @@
     barrier = pltpu.get_barrier_semaphore()
     peers = NZ - 1 + ny - 1 + nkv - 1
     for count, peer_of in ((NZ, z_peer), (ny, y_peer), (nkv, kv_peer)):
-        for d in range(1, count):
+        for d in far_first(count):
             pl.semaphore_signal(barrier, inc=1, device_id=peer_of(d)[1], device_id_type=MESH)
 
     first = lax.div(ctx * out_here, 128) * 128
@@ -86,6 +86,14 @@
     loads = [pltpu.make_async_copy(a, b, in_sem.at[i]) for i, (a, b) in enumerate(loads)]
     for load in loads:
         load.start()
+
+    loads[0].wait()
+    loads[1].wait()
+    proj = nn(hid_v[...], wq_v[...])
+    for j in range(GROUP + 2):
+        for s in range(STEPS):
+            at = s * GROUP + j if j < GROUP else QR + (j - GROUP) * STEPS + s
+            part[pl.ds(at, ROWS, stride=PIECE), :] = proj[s * ROWS:(s + 1) * ROWS, j * HD:(j + 1) * HD]
 
     tk_v[out_here] = jnp.zeros((PAGE, HD), jnp.bfloat16)
     tv_v[out_here] = jnp.zeros((PAGE, HD), jnp.bfloat16)
@@ -106,14 +114,20 @@
     table_copy = pltpu.make_async_copy(inv_v, inv_s, inv_sem.at[0])
     table_copy.start()
 
-    loads[0].wait()
-    loads[1].wait()
-    proj = nn(hid_v[...], wq_v[...])
-    for j in range(GROUP + 2):
-        for s in range(STEPS):
-            at = s * GROUP + j if j < GROUP else QR + (j - GROUP) * STEPS + s
-            part[pl.ds(at, ROWS, stride=PIECE), :] = proj[s * ROWS:(s + 1) * ROWS, j * HD:(j + 1) * HD]
-
+    loads[3].wait()
+    loads[4].wait()
+    table_copy.wait()
+
+    def place(d, carry):
+        to_z = lax.div(d, ny)
+        to_y = lax.rem(d, ny)
+        for k in range(PAIR):
+            page = inv_s[0, d * PAIR + k]
+            stage_k[to_y, to_z, k] = tk_v[page]
+            stage_v[to_z, to_y, k] = tv_v[page]
+        return carry
+
+    lax.fori_loop(0, n_ctx, place, 0)
     pl.semaphore_wait(barrier, peers)
 
     def piece(i):
@@ -124,7 +138,7 @@
 
     def exchange(phase, count, peer_of, me, src, dst, recv):
         copies = []
-        for d in range(1, count):
+        for d in far_first(count):
             peer, device = peer_of(d)
             copy = pltpu.make_async_remote_copy(
                 src_ref=src(peer), dst_ref=dst(me), send_sem=send_sem.at[phase, d], recv_sem=recv.at[me],
@@ -146,7 +160,7 @@
     sent = []
 
     tail_peer = (y_peer, z_peer, z_peer, y_peer)
-    tail_order = (far_first(ny), far_first(NZ), far_first(NZ), far_first(ny))
+    tail_order = ((4, 2, 6, 3, 5, 1, 7), (4, 2, 6, 3, 5, 1, 7), (4, 2, 6, 3, 5, 1, 7), (4, 2, 6, 3, 5, 1, 7))
     tail_src = (
         lambda p: stage_k.at[p], lambda p: stage_v.at[p], lambda p: mid_k.at[:, p], lambda p: mid_v.at[:, p],
     )
@@ -173,20 +187,6 @@
     sent += copies
     ra1[z] = part[piece(z), :]
 
-    loads[3].wait()
-    loads[4].wait()
-    table_copy.wait()
-
-    def place(d, carry):
-        to_z = lax.div(d, ny)
-        to_y = lax.rem(d, ny)
-        for k in range(PAIR):
-            page = inv_s[0, d * PAIR + k]
-            stage_k[to_y, to_z, k] = tk_v[page]
-            stage_v[to_z, to_y, k] = tv_v[page]
-        return carry
-
-    lax.fori_loop(0, n_ctx, place, 0)
     tail_start(0)
 
     wait()
@@ -232,6 +232,7 @@
     loads[7].wait()
     wait()
 
+    tail_start(7)
     q_all = qbuf[...]
     scores_t = nt(q_all, tk_v[pl.ds(0, out_here)].reshape(tail_tokens, HD)) * score_scale
     q_row = lax.shift_right_logical(lax.broadcasted_iota(jnp.int32, (ROWS * QR, tail_tokens), 0), 4)
@@ -248,23 +249,29 @@
     weights_t = jnp.exp(scores_t - jnp.concatenate(peaks, axis=0))
     sums_t = jnp.sum(weights_t, axis=1, keepdims=True)
     out_t = nn(weights_t.astype(jnp.bfloat16), tv_v[pl.ds(0, out_here)].reshape(tail_tokens, HD))
-    lane8 = lax.broadcasted_iota(jnp.int32, (8, HD), 1)
+    lanes = lax.broadcasted_iota(jnp.int32, (QR, HD), 1)
+
+    def parts(v):
+        high = v.astype(jnp.bfloat16).astype(jnp.float32)
+        middle = (v - high).astype(jnp.bfloat16).astype(jnp.float32)
+        return high, middle, v - high - middle
 
     def pack(m, l):
-        return jnp.where(
-            lane8 < 32, m[:8], jnp.where(lane8 < 64, m[8:], jnp.where(lane8 < 96, l[:8], l[8:]))
-        )
+        tile = jnp.zeros((QR, HD), jnp.float32)
+        for i, part_of in enumerate(parts(m) + parts(l)):
+            tile = jnp.where(lanes == i, part_of, tile)
+        return tile.astype(jnp.bfloat16)
 
     for r in range(ROWS):
         weights_r = jnp.exp(scores_r[r] - peaks[r])
         sums = jnp.sum(weights_r, axis=1, keepdims=True) + sums_t[r * QR:(r + 1) * QR]
         out_r = nn(weights_r.astype(jnp.bfloat16), v_v[r]) + out_t[r * QR:(r + 1) * QR]
-        bsend[pl.ds(r * PIECE, QR), :] = out_r
-        bsend[pl.ds(r * PIECE + QR, 8), :] = pack(peaks[r], sums)
-
-    wait, copies = exchange(3, ny, y_peer, y, lambda p: bsend.at[piece(p)], lambda m: rb1.at[m], yb_sem)
-    sent += copies
-    rb1[y] = bsend[piece(y), :]
+        bsend[r, pl.ds(0, QR), :] = out_r.astype(jnp.bfloat16)
+        bsend[r, pl.ds(QR, QR), :] = pack(peaks[r], sums)
+
+    wait, copies = exchange(3, ny, y_peer, y, lambda p: bsend.at[p], lambda m: rb1.at[m], yb_sem)
+    sent += copies
+    rb1[y] = bsend[y]
     tail_start(3)
 
     q_f = my_q.astype(jnp.float32)
@@ -275,10 +282,10 @@
     own_scores = [jnp.where((step_of >= u) & (z == y), own_scores[u], NEG) for u in range(STEPS)]
 
     def merge(ref, count):
-        tiles = [ref[i, pl.ds(QR, 8), :] for i in range(count)]
-        ms = [jnp.concatenate([t[:, 0:1], t[:, 32:33]], axis=0) for t in tiles]
-        ls = [jnp.concatenate([t[:, 64:65], t[:, 96:97]], axis=0) for t in tiles]
-        return ms, ls, [ref[i, pl.ds(0, QR), :] for i in range(count)]
+        tiles = [ref[i, pl.ds(QR, QR), :].astype(jnp.float32) for i in range(count)]
+        ms = [t[:, 0:1] + t[:, 1:2] + t[:, 2:3] for t in tiles]
+        ls = [t[:, 3:4] + t[:, 4:5] + t[:, 5:6] for t in tiles]
+        return ms, ls, [ref[i, pl.ds(0, QR), :].astype(jnp.float32) for i in range(count)]
 
     def combine(ms, ls, os, m):
         factors = [jnp.exp(a - m) for a in ms]
@@ -294,8 +301,8 @@
     for u, w in enumerate(own):
         l = l + w
         o = o + w.astype(jnp.bfloat16).astype(jnp.float32) * new_kv[STEPS + u:STEPS + u + 1]
-    b2s[pl.ds(0, QR), :] = o
-    b2s[pl.ds(QR, 8), :] = pack(peak, l)
+    b2s[pl.ds(0, QR), :] = o.astype(jnp.bfloat16)
+    b2s[pl.ds(QR, QR), :] = pack(peak, l)
     wait, copies = exchange(4, NZ, z_peer, z, lambda p: b2s, lambda m: rb2.at[m], zb_sem)
     sent += copies
     rb2[z] = b2s[...]
@@ -398,10 +405,10 @@
             pltpu.VMEM((QR, HD), bf),
             pltpu.VMEM((ROWS * QR, HD), bf),
             pltpu.VMEM((ROWS * STEPS, tokens), f32),
-            pltpu.VMEM((ROWS * PIECE, HD), f32),
-            pltpu.VMEM((ny, PIECE, HD), f32),
-            pltpu.VMEM((PIECE, HD), f32),
-            pltpu.VMEM((NZ, PIECE, HD), f32),
+            pltpu.VMEM((ROWS, 2 * QR, HD), bf),
+            pltpu.VMEM((ny, 2 * QR, HD), bf),
+            pltpu.VMEM((2 * QR, HD), bf),
+            pltpu.VMEM((NZ, 2 * QR, HD), bf),
             pltpu.VMEM((QR, HD), bf),
             pltpu.VMEM((ROWS * QR, HD), bf),
             pltpu.VMEM((ROWS * QR, HD), f32),

time: 63.3 us -> 56.7 us (0.90)
  the two profiles are of different devices: /device:TPU:1 before, /device:TPU:6 now
where the time goes in v3:
time: 56.7 us; the launch traced here: 56.6 us
  Pallas kernels  55.9 us (99%)
  between operations  0.64 us (1%)
    pallas_call x1, Pallas kernels, on_device(): pl.pallas_call(functools.partial(body, ny, nkv, out_here, pages_here), ou...  54.3 us
    pallas_call x1, Pallas kernels, on_device(): pl.pallas_call(functools.partial(store_body, NZ), out_shape=(jax.ShapeDty...  1.62 us

profile of v3, /device:TPU:6, one launch (start us, length us, event | category | flops | bytes accessed | tf_op | source)
XLA Modules:
  0.0 56.6 jit_solution(6182014905947568927)
XLA Ops:
  0.6 54.3 %shard_map.138 = (bf16[16,128]{1,0:T(8,128)(2,1)S(1)}, bf16[8,8,2,16,128]{4,3,2,1,0:T(8,128)(2,1)S(1)}, bf16[8,8,2,16,128]{4,3,2,1,0:T(8,128)(2,1)S(1)}) custom-call(s32[8]{0:T(128)} %ctx_len.1, s32[8]{0:T(128)} %tail_count.1, bf16[16,128]{1,0:T(8,128)(2,1)} %bitcast.10, bf16[128,1280]{1,0:T(8,128)(2,1)} %w_qkv.1, bf16[1024,128]{1,0:T(8,128)(2,1)} %w_out.1, ...), custom_call_target="tpu_custom_call" | custom-call | tf_op jit(solution)/shard_map/pallas_call | solution.py:382
  55.0 1.6 %shard_map.139 = (bf16[16,128]{1,0:T(8,128)(2,1)}, bf16[8,8,2,16,128]{4,3,2,1,0:T(8,128)(2,1)}, bf16[8,8,2,16,128]{4,3,2,1,0:T(8,128)(2,1)}, bf16[128,2,128]{2,1,0:T(2,128)(2,1)}) custom-call(bf16[16,128]{1,0:T(8,128)(2,1)S(1)} %get-tuple-element.11.rows, bf16[8,8,2,16,128]{4,3,2,1,0:T(8,128)(2,1)S(1)} %get-tuple-element.12.got_k, ...), custom_call_target="tpu_custom_call" | custom-call | tf_op jit(solution)/shard_map/pallas_call | solution.py:444

commit v4 on v3

--- a/solution.py
+++ b/solution.py
@@ -19,7 +19,10 @@
 PIECE = 24
 NEG = -1e30
 MESH = pl.DeviceIdType.MESH
-SCHEDULE = (((0, 3),), ((1, 3),), ((0, 4),), ((1, 4),), ((3, 3),), ((2, 3),), ((2, 4), (3, 4)), ())
+SCHEDULE = (((0, 3),), ((1, 3),), ((0, 4),), ((1, 4),), ((3, 3),), ((2, 3),), ((3, 1), (2, 1), (3, 1), (2, 1), (3, 1), (2, 1), (3, 1), (2, 1)), ())
+
+
+TAIL_ORDER = (4, 1, 7, 3, 5, 2, 6)
 
 
 def far_first(count):
@@ -160,7 +163,7 @@
     sent = []
 
     tail_peer = (y_peer, z_peer, z_peer, y_peer)
-    tail_order = ((4, 2, 6, 3, 5, 1, 7), (4, 2, 6, 3, 5, 1, 7), (4, 2, 6, 3, 5, 1, 7), (4, 2, 6, 3, 5, 1, 7))
+    tail_order = (TAIL_ORDER,) * 4
     tail_src = (
         lambda p: stage_k.at[p], lambda p: stage_v.at[p], lambda p: mid_k.at[:, p], lambda p: mid_v.at[:, p],
     )
@@ -329,10 +332,12 @@
     sent += copies
     rc[kv] = mine
     tail_start(6)
+    for copy in sent[:-len(copies)]:
+        copy.wait_send()
     wait()
     mixed[...] = functools.reduce(lambda a, b: a + b, [rc[i] for i in range(nkv)]).astype(jnp.bfloat16)
 
-    for copy in sent:
+    for copy in copies:
         copy.wait_send()
     for kind in (2, 3):
         pltpu.make_async_copy(landing[kind], landing[kind], tail_recv.at[kind]).wait()

time: 56.7 us -> 55.1 us (0.972)
  Pallas kernels: 55.9 us -> 54.3 us
    pallas_call x1, Pallas kernels: 54.3 us -> 52.7 us  [on_device(): pl.pallas_call(functools.partial(body, ny, nkv, out_here, pages_here), ou...]
where the time goes in v4:
time: 55.1 us; the launch traced here: 55 us
  Pallas kernels  54.3 us (99%)
  between operations  0.64 us (1%)
    pallas_call x1, Pallas kernels, on_device(): pl.pallas_call(functools.partial(body, ny, nkv, out_here, pages_here), ou...  52.7 us
    pallas_call x1, Pallas kernels, on_device(): pl.pallas_call(functools.partial(store_body, NZ), out_shape=(jax.ShapeDty...  1.62 us

profile of v4, /device:TPU:6, one launch (start us, length us, event | category | flops | bytes accessed | tf_op | source)
XLA Modules:
  0.0 55.0 jit_solution(7970957448819417515)
XLA Ops:
  0.6 52.7 %shard_map.138 = (bf16[16,128]{1,0:T(8,128)(2,1)S(1)}, bf16[8,8,2,16,128]{4,3,2,1,0:T(8,128)(2,1)S(1)}, bf16[8,8,2,16,128]{4,3,2,1,0:T(8,128)(2,1)S(1)}) custom-call(s32[8]{0:T(128)} %ctx_len.1, s32[8]{0:T(128)} %tail_count.1, bf16[16,128]{1,0:T(8,128)(2,1)} %bitcast.10, bf16[128,1280]{1,0:T(8,128)(2,1)} %w_qkv.1, bf16[1024,128]{1,0:T(8,128)(2,1)} %w_out.1, ...), custom_call_target="tpu_custom_call" | custom-call | tf_op jit(solution)/shard_map/pallas_call | solution.py:387
  53.3 1.6 %shard_map.139 = (bf16[16,128]{1,0:T(8,128)(2,1)}, bf16[8,8,2,16,128]{4,3,2,1,0:T(8,128)(2,1)}, bf16[8,8,2,16,128]{4,3,2,1,0:T(8,128)(2,1)}, bf16[128,2,128]{2,1,0:T(2,128)(2,1)}) custom-call(bf16[16,128]{1,0:T(8,128)(2,1)S(1)} %get-tuple-element.11.rows, bf16[8,8,2,16,128]{4,3,2,1,0:T(8,128)(2,1)S(1)} %get-tuple-element.12.got_k, ...), custom_call_target="tpu_custom_call" | custom-call | tf_op jit(solution)/shard_map/pallas_call | solution.py:449

commit v5 on v4

--- a/solution.py
+++ b/solution.py
@@ -19,7 +19,7 @@
 PIECE = 24
 NEG = -1e30
 MESH = pl.DeviceIdType.MESH
-SCHEDULE = (((0, 3),), ((1, 3),), ((0, 4),), ((1, 4),), ((3, 3),), ((2, 3),), ((3, 1), (2, 1), (3, 1), (2, 1), (3, 1), (2, 1), (3, 1), (2, 1)), ())
+SCHEDULE = (((0, 3),), ((1, 3),), ((0, 3),), ((1, 3),), ((3, 3),), ((2, 3),), ((3, 1), (2, 1), (3, 1), (2, 1), (3, 1), (2, 1), (3, 1), (2, 1)), ((0, 1), (1, 1)))
 
 
 TAIL_ORDER = (4, 1, 7, 3, 5, 2, 6)

time: 55.1 us -> 55.2 us (level)
  the two profiles are of different devices: /device:TPU:6 before, /device:TPU:1 now
where the time goes in v5:
time: 55.2 us; the launch traced here: 54.4 us
  Pallas kernels  53.7 us (97%)
  between operations  0.64 us (1%)
    pallas_call x1, Pallas kernels, on_device(): pl.pallas_call(functools.partial(body, ny, nkv, out_here, pages_here), ou...  52.1 us
    pallas_call x1, Pallas kernels, on_device(): pl.pallas_call(functools.partial(store_body, NZ), out_shape=(jax.ShapeDty...  1.62 us

profile of v5, /device:TPU:1, one launch (start us, length us, event | category | flops | bytes accessed | tf_op | source)
XLA Modules:
  0.0 54.4 jit_solution(15572895971852323917)
XLA Ops:
  0.6 52.1 %shard_map.138 = (bf16[16,128]{1,0:T(8,128)(2,1)S(1)}, bf16[8,8,2,16,128]{4,3,2,1,0:T(8,128)(2,1)S(1)}, bf16[8,8,2,16,128]{4,3,2,1,0:T(8,128)(2,1)S(1)}) custom-call(s32[8]{0:T(128)} %ctx_len.1, s32[8]{0:T(128)} %tail_count.1, bf16[16,128]{1,0:T(8,128)(2,1)} %bitcast.10, bf16[128,1280]{1,0:T(8,128)(2,1)} %w_qkv.1, bf16[1024,128]{1,0:T(8,128)(2,1)} %w_out.1, ...), custom_call_target="tpu_custom_call" | custom-call | tf_op jit(solution)/shard_map/pallas_call | solution.py:387
  52.7 1.6 %shard_map.139 = (bf16[16,128]{1,0:T(8,128)(2,1)}, bf16[8,8,2,16,128]{4,3,2,1,0:T(8,128)(2,1)}, bf16[8,8,2,16,128]{4,3,2,1,0:T(8,128)(2,1)}, bf16[128,2,128]{2,1,0:T(2,128)(2,1)}) custom-call(bf16[16,128]{1,0:T(8,128)(2,1)S(1)} %get-tuple-element.11.rows, bf16[8,8,2,16,128]{4,3,2,1,0:T(8,128)(2,1)S(1)} %get-tuple-element.12.got_k, ...), custom_call_target="tpu_custom_call" | custom-call | tf_op jit(solution)/shard_map/pallas_call | solution.py:449
